TPU v7x, 1024 devices: a whole 8x8x8 slice. The times are simulated.
1024 devices in a mesh: dp: 128 (over x, y, z_lo), expert: 8 (over z_hi, core).
Axes of the slice: x: 8, y: 8, z: 8 (z_hi: 4, z_lo: 2; z = z_hi * 2 + z_lo), core: 2. Of those that a mesh axis runs over, the one named last changes fastest.
Arguments:
- grad_out: bfloat16 [131072, 2048], P(('dp', 'expert')), may hold values from -1.5 to 1.5
- expert_ids: int32 [131072, 2], P(('dp', 'expert')), may hold values from 0 to 7, all different within a row; in each aligned block of 128 rows (0 to 127, 128 to 255, ...) at most 40 rows name the same one
- gate_probs: bfloat16 [131072, 2], P(('dp', 'expert')), may hold values from 0.099609375 to 1
- hidden_saved: bfloat16 [8, 128, 8, 40, 768], P('expert', 'dp'), may hold values from -24 to 24
- w_down: bfloat16 [8, 768, 2048], P('expert'), may hold values from -0.21875 to 0.21875
Outputs:
- grad_hidden: bfloat16 [131072, 2, 768], P(('dp', 'expert'))
- grad_gate: bfloat16 [131072, 2], P(('dp', 'expert'))
- weight_grad: float32 [8, 768, 2048], P('expert', 'dp')
Inputs may be any that keep to these rules, and one draw needn't show every extreme that they name: `expert_ids`: each token names 2 different experts; among the tokens of one device no expert is named more than 40 times, a bound that some block reaches.
All inputs are finite; a program needn't handle non-finite values.
Results may differ from a plain program's by a relative error of at most 0.0049.
Values may be sent and summed in bfloat16 or wider, within the bound.
A program may use at most 64 MiB of HBM per device.

v0:
```python
import jax
import jax.numpy as jnp
from jax import lax
from jax.sharding import PartitionSpec as P


def body(grad_out, expert_ids, gate_probs, hidden_saved, w_down):
    tok_rows, model_width = grad_out.shape
    top_picks = expert_ids.shape[1]
    local_experts = w_down.shape[0]
    hidden_units = w_down.shape[1]
    groups = lax.axis_size("expert")
    capacity = hidden_saved.shape[3]
    routed = tok_rows * top_picks
    flat_ids = expert_ids.reshape(routed)
    onehot = (
        flat_ids[:, None] == jnp.arange(local_experts * groups, dtype=jnp.int32)[None, :]
    ).astype(jnp.int32)
    slot_of = jnp.sum((jnp.cumsum(onehot, axis=0) - 1) * onehot, axis=1)
    owner_group = flat_ids // local_experts
    within = flat_ids % local_experts
    target = (within * groups + owner_group) * capacity + slot_of
    token_of = jnp.arange(routed, dtype=jnp.int32) // top_picks
    total_slots = local_experts * groups * capacity
    outgoing = (
        jnp.zeros((total_slots, model_width), jnp.bfloat16).at[target].set(grad_out[token_of])
    )
    gate_slots = jnp.zeros((total_slots,), jnp.bfloat16).at[target].set(gate_probs.reshape(routed))
    outgoing = outgoing.reshape(local_experts, groups, capacity, model_width)
    gate_slots = gate_slots.reshape(local_experts, groups, capacity)
    arrived, arrived_gates = (
        lax.all_to_all(outgoing, "expert", split_axis=1, concat_axis=1, tiled=True),
        lax.all_to_all(gate_slots, "expert", split_axis=1, concat_axis=1, tiled=True),
    )
    saved_rows = hidden_saved.reshape(local_experts, groups * capacity, hidden_units)
    rows_in = arrived.reshape(local_experts, groups * capacity, model_width)
    gates_in = arrived_gates.reshape(local_experts, groups * capacity).astype(jnp.float32)
    recomputed = jnp.einsum("erf,efd->erd", saved_rows, w_down, preferred_element_type=jnp.float32)
    gate_grad = jnp.sum(rows_in.astype(jnp.float32) * recomputed, axis=2).astype(jnp.bfloat16)
    scaled = (gates_in[:, :, None] * rows_in.astype(jnp.float32)).astype(jnp.bfloat16)
    hidden_grad = jnp.einsum(
        "erd,efd->erf", scaled, w_down, preferred_element_type=jnp.float32
    ).astype(jnp.bfloat16)
    partial_all = jnp.einsum("erf,erd->fed", saved_rows, scaled, preferred_element_type=jnp.float32)
    summed = lax.psum_scatter(partial_all, "dp", scatter_dimension=0, tiled=True)
    weight_grad = jnp.transpose(summed, (1, 0, 2))
    back_rows, back_gate = (
        lax.all_to_all(
            hidden_grad.reshape(local_experts, groups, capacity, hidden_units),
            "expert",
            split_axis=1,
            concat_axis=1,
            tiled=True,
        ),
        lax.all_to_all(
            gate_grad.reshape(local_experts, groups, capacity),
            "expert",
            split_axis=1,
            concat_axis=1,
            tiled=True,
        ),
    )
    grad_hidden = back_rows.reshape(total_slots, hidden_units)[target].reshape(
        tok_rows, top_picks, hidden_units
    )
    grad_gate = back_gate.reshape(total_slots)[target].reshape(tok_rows, top_picks)
    return (grad_hidden, grad_gate, weight_grad)


def solution(mesh):
    in_specs = (
        P(("dp", "expert"), None),
        P(("dp", "expert"), None),
        P(("dp", "expert"), None),
        P("expert", "dp", None, None, None),
        P("expert", None, None),
    )
    out_specs = (
        P(("dp", "expert"), None, None),
        P(("dp", "expert"), None),
        P("expert", "dp", None),
    )
    return jax.shard_map(body, mesh=mesh, in_specs=in_specs, out_specs=out_specs, check_vma=False)
```

profile of v0, /device:TPU:8, one launch (start us, length us, event | category | flops | bytes accessed | tf_op | source)
XLA Modules:
  0.0 1333.1 jit_solution(11372428771793398047)
XLA Ops:
  7.2 0.8 broadcast_multiply_fusion
  8.0 0.9 copy.23
  11.4 2.2 scatter_custom_fusion
  14.2 15.8 %all-to-all-start = ((bf16[1,8,40]{2,0,1:T(2,128)(2,1)}), bf16[1,8,40]{2,0,1:T(2,128)(2,1)S(1)}, u32[]{:S(2)}, u32[]{:S(2)}) async-start(bf16[1,8,40]{2,0,1:T(2,128)(2,1)} %reshape.290), calls=%async_computation | async-start | bytes 8192 | tf_op jit(solution)/shard_map/all_to_all | solution.py:33
  30.0 6.8 scatter_custom_fusion.1
  36.8 0.8 all-to-all-done
  37.6 6.4 all-to-all-start.1
  44.1 35.2 %all-to-all-done.1 = bf16[1,8,40,2048]{3,2,0,1:T(8,128)(2,1)} async-done(((bf16[1,8,40,2048]{3,2,0,1:T(8,128)(2,1)}), bf16[1,8,40,2048]{3,2,0,1:T(8,128)(2,1)}, u32[]{:S(2)}, u32[]{:S(2)}) %all-to-all-start.1) | async-done | bytes 1310752 | tf_op jit(solution)/shard_map/all_to_all | solution.py:32
  79.3 1.7 convert_element_type.108
  81.0 1.5 copy-done.1
  82.5 4.6 convolution_bitcast_fusion
  87.1 15.9 %copy.29 = f32[768,1,2048]{2,1,0:T(1,128)} copy(f32[768,1,2048]{0,2,1:T(8,128)} %convolution_bitcast_fusion) | data formatting | bytes 12582912 | tf_op jit(solution)/shard_map/erf,erd->fed/transpose | solution.py:44
  103.0 3.2 fusion.7
  106.9 3.5 all-to-all-start.3
  110.4 3.8 fusion.11
  114.2 3.6 all-to-all-done.3
  117.8 4.1 all-to-all-start.2
  121.9 1.3 dynamic-slice
  124.0 1.9 gather_fusion.1
  126.7 15.9 %all-to-all-done.2 = bf16[1,8,40,768]{3,2,0,1:T(8,128)(2,1)} async-done(((bf16[1,8,40,768]{3,2,0,1:T(8,128)(2,1)}), bf16[1,8,40,768]{3,2,0,1:T(8,128)(2,1)}, u32[]{:S(2)}, u32[]{:S(2)}) %all-to-all-start.2) | async-done | bytes 491552 | tf_op jit(solution)/shard_map/all_to_all | solution.py:48
  142.6 2.5 gather_fusion
  145.1 0.9 reshape.243
  146.0 1178.9 %all-reduce.3.cloned.1.call-done = f32[768,1,2048]{2,1,0:T(1,128)} async-done(((f32[768,1,2048]{2,1,0:T(1,128)}), f32[768,1,2048]{2,1,0:T(1,128)}) %all-reduce.3.cloned.1.call-update) | async-done | bytes 6291472
  1324.9 1.4 dynamic-slice_bitcast_fusion
  (31 shorter events, 4.8 us)
Async XLA Ops:
  7.2 95.9 %copy-start = (bf16[1,768,2048]{2,1,0:T(8,128)(2,1)S(1)}, bf16[1,768,2048]{2,1,0:T(8,128)(2,1)}, u32[]{:S(2)}) copy-start(bf16[1,768,2048]{2,1,0:T(8,128)(2,1)} %param.9) | copy-start | bytes 9437188
  14.2 23.4 %all-to-all-start = ((bf16[1,8,40]{2,0,1:T(2,128)(2,1)}), bf16[1,8,40]{2,0,1:T(2,128)(2,1)S(1)}, u32[]{:S(2)}, u32[]{:S(2)}) async-start(bf16[1,8,40]{2,0,1:T(2,128)(2,1)} %reshape.290), calls=%async_computation | async-start | bytes 8192 | tf_op jit(solution)/shard_map/all_to_all | solution.py:33
  37.6 41.7 %all-to-all-start.1 = ((bf16[1,8,40,2048]{3,2,0,1:T(8,128)(2,1)}), bf16[1,8,40,2048]{3,2,0,1:T(8,128)(2,1)}, u32[]{:S(2)}, u32[]{:S(2)}) async-start(bf16[1,8,40,2048]{3,2,0,1:T(8,128)(2,1)} %bitcast.44), calls=%async_computation.1 | async-start | bytes 2621440 | tf_op jit(solution)/shard_map/all_to_all | solution.py:32
  44.0 1280.9 %all-reduce.3.cloned.1.call-start = ((), (), s32[]{:S(2)}) async-start(), calls=%async_computation.4 | async-start | bytes 12582912
  79.3 3.2 copy-start.2
  81.0 1.5 copy-start.1
  106.9 10.8 all-to-all-start.3
  117.8 24.8 %all-to-all-start.2 = ((bf16[1,8,40,768]{3,2,0,1:T(8,128)(2,1)}), bf16[1,8,40,768]{3,2,0,1:T(8,128)(2,1)}, u32[]{:S(2)}, u32[]{:S(2)}) async-start(bf16[1,8,40,768]{3,2,0,1:T(8,128)(2,1)} %bitcast.47), calls=%async_computation.2 | async-start | bytes 983040 | tf_op jit(solution)/shard_map/all_to_all | solution.py:48
Sparse Core Ops, SparseCore 0:
  103.1 1221.6 all-reduce.2
where the time goes:
time: 1330 us
  waiting for transfers between devices  1230 us (92%)
  local copies, waits for them, and re-layouts  39.3 us (3%)
  starting transfers between devices  29.8 us (2%)
  between operations  14.8 us (1%)
    unnamed x2, waiting for transfers between devices  1180 us
    all_to_all x1, waiting for transfers between devices, body(): lax.all_to_all(outgoing, 'expert', split_axis=1, concat_axis=1, tiled=True)  35.2 us
  transfers between devices with their start and end apart: 5, of which 5 were waited for; matrix products, arithmetic and copies ran while one was open for 2% of the time, Pallas kernels for 0%

commit v1 on v0

v1 whole, which is shorter than its diff:
```python
import functools

import jax
import jax.numpy as jnp
from jax import lax
from jax.experimental import pallas as pl
from jax.experimental.pallas import tpu as pltpu
from jax.sharding import PartitionSpec as P

MESH = pl.DeviceIdType.MESH
NX, NY, NZ = 8, 8, 2
NE, CAP, TOK, D, FF = 8, 40, 128, 2048, 768
ROWS = NE * CAP
NC = 8
DC = D // NC
H = DC // 2
FH = FF // 2
WINDOW = 2
LAG1, LAG2, LAG3 = 1, 2, 3
F32, BF16 = jnp.float32, jnp.bfloat16
NT = (((1,), (1,)), ((), ()))


def wait_bytes(ref, sem):
    pltpu.make_async_copy(ref, ref, sem).wait()


def fold(block, width):
    left = block[:, :width].reshape(NE, CAP, width)
    right = block[:, width:].reshape(NE, CAP, width)
    return jnp.concatenate([left, right], axis=1).astype(BF16)


def unfold(block, width):
    block = block.astype(F32)
    left = block[:, :CAP, :].reshape(ROWS, width)
    right = block[:, CAP:, :].reshape(ROWS, width)
    return jnp.concatenate([left, right], axis=1).astype(BF16)


def kernel(
    ids_ref, gate_ref, go_ref, hid_hbm, w_hbm,
    gh_ref, gg_ref, wg_ref,
    hid, w, place, picked, hid_t, send, recv, grad, part, r1, q2, r2, tot, r3,
    back, back_in, gate_out, gate_in,
    local, fwd_s, fwd_r, s1_s, s1_r, s2_s, s2_r, s3_s, s3_r, ret_s, ret_r, gs, gr,
):
    dp = lax.axis_index("dp")
    me = lax.axis_index("expert")
    core = lax.rem(me, 2)
    x, y, zl = dp // (NY * NZ), lax.rem(dp // NZ, NY), lax.rem(dp, NZ)
    first = jnp.where(core == 0, x, y)
    second = jnp.where(core == 0, y, x)

    def peer(k):
        return lax.rem(me + k, NE)

    def along(sx, sy):
        return (lax.rem(x + sx, NX) * NY + lax.rem(y + sy, NY)) * NZ + zl

    def dev1(k):
        return (along(k * (1 - core), k * core), me)

    def dev2(k):
        return (along(k * core, k * (1 - core)), me)

    dev3 = (dp + 1 - 2 * zl, me)

    barrier = pltpu.get_barrier_semaphore()

    def greet(k, _):
        for device in ((dp, peer(k)), dev1(k), dev2(k)):
            pl.semaphore_signal(barrier, inc=1, device_id=device, device_id_type=MESH)
        return 0

    lax.fori_loop(1, 8, greet, 0)
    pl.semaphore_signal(barrier, inc=1, device_id=dev3, device_id_type=MESH)

    load_hid = pltpu.make_async_copy(hid_hbm, hid, local.at[0])
    load_w = pltpu.make_async_copy(w_hbm, w, local.at[1])
    load_hid.start()
    load_w.start()

    ids = ids_ref[...]
    gates = gate_ref[...].astype(F32)
    expert = lax.broadcasted_iota(jnp.int32, (NE, TOK), 0)
    chosen = [ids[k : k + 1] == expert for k in range(2)]
    named = jnp.where(chosen[0] | chosen[1], 1.0, 0.0)
    before = (
        lax.broadcasted_iota(jnp.int32, (TOK, TOK), 0) < lax.broadcasted_iota(jnp.int32, (TOK, TOK), 1)
    )
    slot = jnp.dot(
        named.astype(BF16), jnp.where(before, 1.0, 0.0).astype(BF16), preferred_element_type=F32
    )
    row = lax.broadcasted_iota(jnp.int32, (CAP, TOK), 0).astype(F32)
    spots = []
    for k in range(2):
        own = jnp.where(chosen[k], slot, -1.0)
        spots.append(
            jnp.concatenate(
                [jnp.where(row == own[e : e + 1], 1.0, 0.0) for e in range(NE)], axis=0
            )
        )
    place[...] = (spots[0] * gates[0:1] + spots[1] * gates[1:2]).astype(BF16)

    def dispatch(c):
        columns = go_ref[:, pl.ds(pl.multiple_of(c * DC, DC), DC)]
        rows = jnp.dot(place[...], columns, preferred_element_type=F32)
        send[c] = fold(rows, H)
        recv[c, me] = send[c, me]

    def forward(c):
        def one(k, _):
            pltpu.make_async_remote_copy(
                src_ref=send.at[c, peer(k)], dst_ref=recv.at[c, me],
                send_sem=fwd_s.at[c], recv_sem=fwd_r.at[c],
                device_id=(dp, peer(k)), device_id_type=MESH,
            ).start()
            return 0

        lax.fori_loop(1, NE, one, 0)

    dispatch(0)
    pl.semaphore_wait(barrier, 22)
    forward(0)

    def prepare(c, _):
        dispatch(c)

        @pl.when(c < WINDOW)
        def _():
            forward(c)

        return 0

    lax.fori_loop(1, NC, prepare, 0)

    eye = (
        lax.broadcasted_iota(jnp.int32, (TOK, TOK), 0) == lax.broadcasted_iota(jnp.int32, (TOK, TOK), 1)
    )
    eye = jnp.where(eye, 1.0, 0.0).astype(BF16)
    for k in range(2):
        picked[k] = lax.dot_general(
            eye, spots[k].astype(BF16), NT, preferred_element_type=F32
        ).astype(BF16)

    j = lax.broadcasted_iota(jnp.int32, (FF, 1), 0)
    major = (j * 683) >> 16
    rest = j - 96 * major
    minor = (rest * 171) >> 11
    turned = minor * 96 + major * 12 + (rest - 12 * minor)
    source = jnp.where(core == 0, j, turned)
    order = jnp.where(lax.broadcasted_iota(jnp.int32, (FF, FF), 1) == source, 1.0, 0.0).astype(BF16)
    load_hid.wait()
    hid_t[...] = lax.dot_general(order, hid[...], NT, preferred_element_type=F32).astype(BF16)
    grad[...] = jnp.zeros_like(grad)

    i = lax.broadcasted_iota(jnp.int32, (128, 1), 0)
    inner = i & 7
    origin = (i >> 4) * 12 + ((i >> 3) & 1) * 6 + inner
    spread = lax.broadcasted_iota(jnp.int32, (128, 96), 1) == jnp.where(inner < 6, origin, -1)
    spread = jnp.where(spread, 1.0, 0.0).astype(BF16)
    load_w.wait()

    def step(c, _):
        @pl.when(c < NC)
        def _():
            wait_bytes(recv.at[c, pl.ds(0, NE - 1)], fwd_r.at[c])

            @pl.when(c + WINDOW < NC)
            def _():
                forward(c + WINDOW)

            rows = unfold(recv[c], H)
            part[c] = (
                jnp.dot(hid_t[...], rows, preferred_element_type=F32).astype(BF16).reshape(8, 96, DC)
            )

            def one(k, _):
                pltpu.make_async_remote_copy(
                    src_ref=part.at[c, lax.rem(first + k, 8)], dst_ref=r1.at[c, k - 1],
                    send_sem=s1_s.at[c], recv_sem=s1_r.at[c],
                    device_id=dev1(k), device_id_type=MESH,
                ).start()
                return 0

            lax.fori_loop(1, 8, one, 0)
            columns = w[:, pl.ds(pl.multiple_of(c * DC, DC), DC)]
            grad[...] += lax.dot_general(rows, columns, NT, preferred_element_type=F32)

        @pl.when(c == NC - 1)
        def _():
            total = grad[...]
            gate_sum = jnp.sum(hid[...].astype(F32) * total, axis=1, keepdims=True)
            shape = (NE, CAP, 128)
            diagonal = lax.broadcasted_iota(jnp.int32, shape, 1) == lax.broadcasted_iota(jnp.int32, shape, 2)
            flat = jnp.sum(
                jnp.where(diagonal, gate_sum.reshape(NE, CAP, 1), 0.0), axis=1, keepdims=True
            )
            gate_out[...] = jnp.broadcast_to(flat, (NE, 8, 128))
            back[...] = fold(total, FH)
            back_in[me] = back[me]
            gate_in[me] = gate_out[me]

            def one(k, _):
                pltpu.make_async_remote_copy(
                    src_ref=back.at[peer(k)], dst_ref=back_in.at[me],
                    send_sem=ret_s.at[0], recv_sem=ret_r.at[0],
                    device_id=(dp, peer(k)), device_id_type=MESH,
                ).start()
                pltpu.make_async_remote_copy(
                    src_ref=gate_out.at[peer(k)], dst_ref=gate_in.at[me],
                    send_sem=gs.at[0], recv_sem=gr.at[0],
                    device_id=(dp, peer(k)), device_id_type=MESH,
                ).start()
                return 0

            lax.fori_loop(1, NE, one, 0)

        @pl.when((c >= LAG1) & (c < NC + LAG1))
        def _():
            b = c - LAG1
            wait_bytes(r1.at[b], s1_r.at[b])
            total = part[b, first].astype(F32)
            for k in range(7):
                total += r1[b, k].astype(F32)
            wide = jnp.dot(spread, total.astype(BF16), preferred_element_type=F32)
            q2[b] = wide.astype(BF16).reshape(8, 16, DC)

            def one(k, _):
                pltpu.make_async_remote_copy(
                    src_ref=q2.at[b, lax.rem(second + k, 8)], dst_ref=r2.at[b, k - 1],
                    send_sem=s2_s.at[b], recv_sem=s2_r.at[b],
                    device_id=dev2(k), device_id_type=MESH,
                ).start()
                return 0

            lax.fori_loop(1, 8, one, 0)

        @pl.when((c >= LAG2) & (c < NC + LAG2))
        def _():
            b = c - LAG2
            wait_bytes(r2.at[b], s2_r.at[b])
            total = q2[b, second].astype(F32)
            for k in range(7):
                total += r2[b, k].astype(F32)
            tot[b] = total.reshape(2, 8, DC)
            pltpu.make_async_remote_copy(
                src_ref=tot.at[b, 1 - zl], dst_ref=r3.at[b],
                send_sem=s3_s.at[b], recv_sem=s3_r.at[b],
                device_id=dev3, device_id_type=MESH,
            ).start()

        @pl.when(c >= LAG3)
        def _():
            b = c - LAG3
            wait_bytes(r3.at[b], s3_r.at[b])
            wg_ref[:, pl.ds(pl.multiple_of(b * DC, DC), DC)] = tot[b, zl] + r3[b]

        return 0

    lax.fori_loop(0, NC + LAG3, step, 0)

    wait_bytes(gate_in.at[pl.ds(0, NE - 1)], gr.at[0])
    wait_bytes(back_in.at[pl.ds(0, NE - 1)], ret_r.at[0])
    returned = unfold(back_in[...], FH)
    for k in range(2):
        gh_ref[k] = jnp.dot(picked[k], returned, preferred_element_type=F32).astype(BF16)
    shape = (NE, CAP, 128)
    diagonal = lax.broadcasted_iota(jnp.int32, shape, 1) == lax.broadcasted_iota(jnp.int32, shape, 2)
    column = jnp.sum(jnp.where(diagonal, gate_in[:, 0:1, :], 0.0), axis=2, keepdims=True).reshape(ROWS, 1)
    for k in range(2):
        value = jnp.sum(spots[k] * column, axis=0, keepdims=True)
        gg_ref[k : k + 1] = value / gates[k : k + 1]

    def settle(c, _):
        wait_bytes(send.at[c, pl.ds(0, NE - 1)], fwd_s.at[c])
        wait_bytes(part.at[c, pl.ds(0, 7)], s1_s.at[c])
        wait_bytes(q2.at[c, pl.ds(0, 7)], s2_s.at[c])
        wait_bytes(tot.at[c, 0], s3_s.at[c])
        return 0

    lax.fori_loop(0, NC, settle, 0)
    wait_bytes(back.at[pl.ds(0, NE - 1)], ret_s.at[0])
    wait_bytes(gate_out.at[pl.ds(0, NE - 1)], gs.at[0])


def body(grad_out, expert_ids, gate_probs, hidden_saved, w_down):
    vmem = pl.BlockSpec(memory_space=pltpu.VMEM)
    far = pl.BlockSpec(memory_space=pl.ANY)
    dma = pltpu.SemaphoreType.DMA
    gh, gg, wg = pl.pallas_call(
        kernel,
        out_shape=(
            jax.ShapeDtypeStruct((2, TOK, FF), BF16),
            jax.ShapeDtypeStruct((2, TOK), F32),
            jax.ShapeDtypeStruct((8, D), F32),
        ),
        in_specs=[vmem, vmem, vmem, far, far],
        out_specs=(vmem, vmem, vmem),
        scratch_shapes=[
            pltpu.VMEM((ROWS, FF), BF16),
            pltpu.VMEM((FF, D), BF16),
            pltpu.VMEM((ROWS, TOK), BF16),
            pltpu.VMEM((2, TOK, ROWS), BF16),
            pltpu.VMEM((FF, ROWS), BF16),
            pltpu.VMEM((NC, NE, 2 * CAP, H), BF16),
            pltpu.VMEM((NC, NE, 2 * CAP, H), BF16),
            pltpu.VMEM((ROWS, FF), F32),
            pltpu.VMEM((NC, 8, 96, DC), BF16),
            pltpu.VMEM((NC, 7, 96, DC), BF16),
            pltpu.VMEM((NC, 8, 16, DC), BF16),
            pltpu.VMEM((NC, 7, 16, DC), BF16),
            pltpu.VMEM((NC, 2, 8, DC), F32),
            pltpu.VMEM((NC, 8, DC), F32),
            pltpu.VMEM((NE, 2 * CAP, FH), BF16),
            pltpu.VMEM((NE, 2 * CAP, FH), BF16),
            pltpu.VMEM((NE, 8, 128), F32),
            pltpu.VMEM((NE, 8, 128), F32),
            dma((2,)),
            dma((NC,)), dma((NC,)), dma((NC,)), dma((NC,)),
            dma((NC,)), dma((NC,)), dma((NC,)), dma((NC,)),
            dma((1,)), dma((1,)), dma((1,)), dma((1,)),
        ],
        compiler_params=pltpu.CompilerParams(
            collective_id=0, has_side_effects=True, vmem_limit_bytes=48 * 2**20
        ),
        name="routed_backward",
    )(
        expert_ids.T,
        gate_probs.T,
        grad_out,
        hidden_saved.reshape(ROWS, FF),
        w_down.reshape(FF, D),
    )
    grad_hidden = jnp.transpose(gh, (1, 0, 2))
    grad_gate = gg.T.astype(BF16)
    return grad_hidden, grad_gate, wg[:6].reshape(1, 6, D)


def solution(mesh):
    in_specs = (
        P(("dp", "expert"), None),
        P(("dp", "expert"), None),
        P(("dp", "expert"), None),
        P("expert", "dp", None, None, None),
        P("expert", None, None),
    )
    out_specs = (
        P(("dp", "expert"), None, None),
        P(("dp", "expert"), None),
        P("expert", "dp", None),
    )
    return jax.shard_map(body, mesh=mesh, in_specs=in_specs, out_specs=out_specs, check_vma=False)
```

time: 1330 us -> 91.2 us (0.07)
  the two profiles are of different devices: /device:TPU:8 before, /device:TPU:16 now
where the time goes in v1:
time: 91.2 us; the launch traced here: 90.9 us
  Pallas kernels  82.6 us (91%)
  local copies, waits for them, and re-layouts  7.11 us (8%)
    pallas_call x1, Pallas kernels, body(): pl.pallas_call(kernel, out_shape=(jax.ShapeDtypeStruct((2, TOK, FF), BF16...  82.6 us
    unnamed x12, local copies, waits for them, and re-layouts  7.11 us

profile of v1, /device:TPU:16, one launch (start us, length us, event | category | flops | bytes accessed | tf_op | source)
XLA Modules:
  0.0 90.9 jit_solution(5376543410371962030)
XLA Ops:
  0.6 0.0 copy-start
  0.6 1.9 %copy-done = bf16[1,768,2048]{2,1,0:T(8,128)(2,1)S(1)} copy-done((bf16[1,768,2048]{2,1,0:T(8,128)(2,1)S(1)}, bf16[1,768,2048]{2,1,0:T(8,128)(2,1)}, u32[]{:S(2)}) %copy-start) | copy-done | bytes 3145752
  2.5 0.0 copy-start.1
  2.5 1.0 %copy-done.1 = bf16[128,2048]{1,0:T(8,128)(2,1)S(1)} copy-done((bf16[128,2048]{1,0:T(8,128)(2,1)S(1)}, bf16[128,2048]{1,0:T(8,128)(2,1)}, u32[]{:S(2)}) %copy-start.1) | copy-done | bytes 524312
  3.6 0.0 copy-start.2
  3.6 1.0 %copy-done.2 = bf16[1,1,8,40,768]{4,3,2,1,0:T(8,128)(2,1)S(1)} copy-done((bf16[1,1,8,40,768]{4,3,2,1,0:T(8,128)(2,1)S(1)}, bf16[1,1,8,40,768]{4,3,2,1,0:T(8,128)(2,1)}, u32[]{:S(2)}) %copy-start.2) | copy-done | bytes 491544
  4.6 0.0 copy-start.3
  4.6 0.7 copy-done.3
  5.3 0.0 copy-start.4
  5.3 0.7 copy-done.4
  5.9 82.6 %routed_backward.1 = (bf16[2,128,768]{2,1,0:T(8,128)(2,1)S(1)}, f32[2,128]{1,0:T(2,128)S(1)}, f32[8,2048]{1,0:T(8,128)S(1)}) custom-call(s32[2,128]{1,0:T(2,128)S(1)} %bitcast.12, bf16[2,128]{1,0:T(2,128)(2,1)S(1)} %bitcast.13, bf16[128,2048]{1,0:T(8,128)(2,1)S(1)} %copy-done.1, bf16[320,768]{1,0:T(8,128)(2,1)S(1)} %bitcast.10, bf16[768,2048]{1,0:T(8,128)(2,1)S(1)} %bitcast.9), custom_call_target="tpu_custom_call" | custom-call | tf_op jit(solution)/shard_map/routed_backward/pallas_call | solution.py:292
  88.5 1.2 %copy.8 = bf16[128,2,768]{2,1,0:T(2,128)(2,1)} copy(bf16[128,2,768]{2,0,1:T(8,128)(2,1)S(1)} %bitcast.11) | data formatting | bytes 786432
  89.7 0.5 convert_bitcast_fusion
  90.2 0.7 copy.9
  (1 shorter events, 0.0 us)
Async XLA Ops:
  0.6 1.9 %copy-start = (bf16[1,768,2048]{2,1,0:T(8,128)(2,1)S(1)}, bf16[1,768,2048]{2,1,0:T(8,128)(2,1)}, u32[]{:S(2)}) copy-start(bf16[1,768,2048]{2,1,0:T(8,128)(2,1)} %param.9) | copy-start | bytes 9437188
  2.5 1.0 %copy-start.1 = (bf16[128,2048]{1,0:T(8,128)(2,1)S(1)}, bf16[128,2048]{1,0:T(8,128)(2,1)}, u32[]{:S(2)}) copy-start(bf16[128,2048]{1,0:T(8,128)(2,1)} %go_ref.1) | copy-start | bytes 1572868
  3.6 1.0 %copy-start.2 = (bf16[1,1,8,40,768]{4,3,2,1,0:T(8,128)(2,1)S(1)}, bf16[1,1,8,40,768]{4,3,2,1,0:T(8,128)(2,1)}, u32[]{:S(2)}) copy-start(bf16[1,1,8,40,768]{4,3,2,1,0:T(8,128)(2,1)} %param.8) | copy-start | bytes 1474564
  4.6 0.7 copy-start.3
  5.3 0.7 copy-start.4

commit v2 on v1

--- a/solution.py
+++ b/solution.py
@@ -15,8 +15,8 @@
 DC = D // NC
 H = DC // 2
 FH = FF // 2
-WINDOW = 2
-LAG1, LAG2, LAG3 = 1, 2, 3
+NEAR, FAR = 2, 3
+LAG1, LAG2, LAG3, LAG4 = 1, 3, 5, 8
 F32, BF16 = jnp.float32, jnp.bfloat16
 NT = (((1,), (1,)), ((), ()))
 
@@ -39,11 +39,11 @@
 
 
 def kernel(
-    ids_ref, gate_ref, go_ref, hid_hbm, w_hbm,
+    ids_hbm, gate_hbm, go_hbm, hid_hbm, w_hbm,
     gh_ref, gg_ref, wg_ref,
-    hid, w, place, picked, hid_t, send, recv, grad, part, r1, q2, r2, tot, r3,
+    ids_ref, gate_ref, go_ref, hid, w, place, picked, hid_t, send, recv, grad, part, leaf, mid, r1, q2, r2, tot, r3,
     back, back_in, gate_out, gate_in,
-    local, fwd_s, fwd_r, s1_s, s1_r, s2_s, s2_r, s3_s, s3_r, ret_s, ret_r, gs, gr,
+    local, fwd_s, fwd_r, leaf_s, leaf_r, mid_s, s1_r, s2_s, s2_r, s3_s, s3_r, ret_s, ret_r, gs, gr,
 ):
     dp = lax.axis_index("dp")
     me = lax.axis_index("expert")
@@ -59,7 +59,11 @@
         return (lax.rem(x + sx, NX) * NY + lax.rem(y + sy, NY)) * NZ + zl
 
     def dev1(k):
+        k = lax.rem(jnp.int32(k), 8)
         return (along(k * (1 - core), k * core), me)
+
+    def at(k):
+        return lax.rem(first + k + 8, 8)
 
     def dev2(k):
         return (along(k * core, k * (1 - core)), me)
@@ -69,17 +73,25 @@
     barrier = pltpu.get_barrier_semaphore()
 
     def greet(k, _):
-        for device in ((dp, peer(k)), dev1(k), dev2(k)):
+        for device in ((dp, peer(k)), dev2(k)):
             pl.semaphore_signal(barrier, inc=1, device_id=device, device_id_type=MESH)
         return 0
 
     lax.fori_loop(1, 8, greet, 0)
+    for k in (1, 2, 6, 7):
+        pl.semaphore_signal(barrier, inc=1, device_id=dev1(k), device_id_type=MESH)
     pl.semaphore_signal(barrier, inc=1, device_id=dev3, device_id_type=MESH)
 
-    load_hid = pltpu.make_async_copy(hid_hbm, hid, local.at[0])
-    load_w = pltpu.make_async_copy(w_hbm, w, local.at[1])
-    load_hid.start()
-    load_w.start()
+    loads = [
+        pltpu.make_async_copy(source, target, local.at[n])
+        for n, (source, target) in enumerate(
+            ((ids_hbm, ids_ref), (gate_hbm, gate_ref), (go_hbm, go_ref), (hid_hbm, hid), (w_hbm, w))
+        )
+    ]
+    for load in loads:
+        load.start()
+    loads[0].wait()
+    loads[1].wait()
 
     ids = ids_ref[...]
     gates = gate_ref[...].astype(F32)
@@ -103,33 +115,41 @@
         )
     place[...] = (spots[0] * gates[0:1] + spots[1] * gates[1:2]).astype(BF16)
 
+    loads[2].wait()
+
     def dispatch(c):
         columns = go_ref[:, pl.ds(pl.multiple_of(c * DC, DC), DC)]
         rows = jnp.dot(place[...], columns, preferred_element_type=F32)
         send[c] = fold(rows, H)
         recv[c, me] = send[c, me]
 
-    def forward(c):
-        def one(k, _):
-            pltpu.make_async_remote_copy(
-                src_ref=send.at[c, peer(k)], dst_ref=recv.at[c, me],
-                send_sem=fwd_s.at[c], recv_sem=fwd_r.at[c],
-                device_id=(dp, peer(k)), device_id_type=MESH,
-            ).start()
-            return 0
-
-        lax.fori_loop(1, NE, one, 0)
+    def forward(c, hops):
+        for hop in hops:
+            for other in range(2):
+                if (hop, other) == (0, 0):
+                    continue
+                to = 2 * lax.rem(me // 2 + hop, 4) + lax.rem(core + other, 2)
+                pltpu.make_async_remote_copy(
+                    src_ref=send.at[c, to], dst_ref=recv.at[c, me],
+                    send_sem=fwd_s.at[c], recv_sem=fwd_r.at[c],
+                    device_id=(dp, to), device_id_type=MESH,
+                ).start()
 
     dispatch(0)
-    pl.semaphore_wait(barrier, 22)
-    forward(0)
+    pl.semaphore_wait(barrier, 19)
+    forward(0, (2,))
+    forward(0, (1, 3, 0))
 
     def prepare(c, _):
         dispatch(c)
 
-        @pl.when(c < WINDOW)
-        def _():
-            forward(c)
+        @pl.when(c < FAR)
+        def _():
+            forward(c, (2,))
+
+        @pl.when(c < NEAR)
+        def _():
+            forward(c, (1, 3, 0))
 
         return 0
 
@@ -151,7 +171,7 @@
     turned = minor * 96 + major * 12 + (rest - 12 * minor)
     source = jnp.where(core == 0, j, turned)
     order = jnp.where(lax.broadcasted_iota(jnp.int32, (FF, FF), 1) == source, 1.0, 0.0).astype(BF16)
-    load_hid.wait()
+    loads[3].wait()
     hid_t[...] = lax.dot_general(order, hid[...], NT, preferred_element_type=F32).astype(BF16)
     grad[...] = jnp.zeros_like(grad)
 
@@ -160,34 +180,53 @@
     origin = (i >> 4) * 12 + ((i >> 3) & 1) * 6 + inner
     spread = lax.broadcasted_iota(jnp.int32, (128, 96), 1) == jnp.where(inner < 6, origin, -1)
     spread = jnp.where(spread, 1.0, 0.0).astype(BF16)
-    load_w.wait()
+    loads[4].wait()
 
     def step(c, _):
         @pl.when(c < NC)
         def _():
             wait_bytes(recv.at[c, pl.ds(0, NE - 1)], fwd_r.at[c])
 
-            @pl.when(c + WINDOW < NC)
+            @pl.when(c + FAR < NC)
             def _():
-                forward(c + WINDOW)
+                forward(c + FAR, (2,))
+
+            @pl.when(c + NEAR < NC)
+            def _():
+                forward(c + NEAR, (1, 3, 0))
 
             rows = unfold(recv[c], H)
             part[c] = (
                 jnp.dot(hid_t[...], rows, preferred_element_type=F32).astype(BF16).reshape(8, 96, DC)
             )
 
-            def one(k, _):
+            sign = 1 - 2 * lax.rem(c, 2)
+            for owner, via, target in (
+                (-4, -2, leaf.at[c, 0]), (-3, -1, leaf.at[c, 1]), (3, 1, leaf.at[c, 2]),
+                (-1, -1, r1.at[c, 0]), (1, 1, r1.at[c, 1]),
+            ):
                 pltpu.make_async_remote_copy(
-                    src_ref=part.at[c, lax.rem(first + k, 8)], dst_ref=r1.at[c, k - 1],
-                    send_sem=s1_s.at[c], recv_sem=s1_r.at[c],
-                    device_id=dev1(k), device_id_type=MESH,
+                    src_ref=part.at[c, at(sign * owner)], dst_ref=target, send_sem=leaf_s.at[c],
+                    recv_sem=s1_r.at[c] if abs(owner) == 1 else leaf_r.at[c],
+                    device_id=dev1(sign * via + 8), device_id_type=MESH,
                 ).start()
-                return 0
-
-            lax.fori_loop(1, 8, one, 0)
             columns = w[:, pl.ds(pl.multiple_of(c * DC, DC), DC)]
             grad[...] += lax.dot_general(rows, columns, NT, preferred_element_type=F32)
 
+            @pl.when(c == NC - 1)
+            def _():
+                back[...] = fold(grad[...], FH)
+                back_in[me] = back[me]
+
+                def one(k, _):
+                    pltpu.make_async_remote_copy(
+                        src_ref=back.at[peer(k)], dst_ref=back_in.at[me],
+                        send_sem=ret_s.at[0], recv_sem=ret_r.at[0],
+                        device_id=(dp, peer(k)), device_id_type=MESH,
+                    ).start()
+                    return 0
+
+                lax.fori_loop(1, NE, one, 0)
         @pl.when(c == NC - 1)
         def _():
             total = grad[...]
@@ -198,16 +237,9 @@
                 jnp.where(diagonal, gate_sum.reshape(NE, CAP, 1), 0.0), axis=1, keepdims=True
             )
             gate_out[...] = jnp.broadcast_to(flat, (NE, 8, 128))
-            back[...] = fold(total, FH)
-            back_in[me] = back[me]
             gate_in[me] = gate_out[me]
 
             def one(k, _):
-                pltpu.make_async_remote_copy(
-                    src_ref=back.at[peer(k)], dst_ref=back_in.at[me],
-                    send_sem=ret_s.at[0], recv_sem=ret_r.at[0],
-                    device_id=(dp, peer(k)), device_id_type=MESH,
-                ).start()
                 pltpu.make_async_remote_copy(
                     src_ref=gate_out.at[peer(k)], dst_ref=gate_in.at[me],
                     send_sem=gs.at[0], recv_sem=gr.at[0],
@@ -220,9 +252,25 @@
         @pl.when((c >= LAG1) & (c < NC + LAG1))
         def _():
             b = c - LAG1
+            sign = 1 - 2 * lax.rem(b, 2)
+            wait_bytes(leaf.at[b], leaf_r.at[b])
+            far_side = part[b, at(-2 * sign)].astype(F32) + leaf[b, 0].astype(F32) + leaf[b, 1].astype(F32)
+            near_side = part[b, at(2 * sign)].astype(F32) + leaf[b, 2].astype(F32)
+            mid[b, 0] = far_side.astype(BF16)
+            mid[b, 1] = near_side.astype(BF16)
+            for n, owner in enumerate((-2, 2)):
+                pltpu.make_async_remote_copy(
+                    src_ref=mid.at[b, n], dst_ref=r1.at[b, 2 + n],
+                    send_sem=mid_s.at[b], recv_sem=s1_r.at[b],
+                    device_id=dev1(sign * owner + 8), device_id_type=MESH,
+                ).start()
+
+        @pl.when((c >= LAG2) & (c < NC + LAG2))
+        def _():
+            b = c - LAG2
             wait_bytes(r1.at[b], s1_r.at[b])
             total = part[b, first].astype(F32)
-            for k in range(7):
+            for k in range(4):
                 total += r1[b, k].astype(F32)
             wide = jnp.dot(spread, total.astype(BF16), preferred_element_type=F32)
             q2[b] = wide.astype(BF16).reshape(8, 16, DC)
@@ -237,9 +285,9 @@
 
             lax.fori_loop(1, 8, one, 0)
 
-        @pl.when((c >= LAG2) & (c < NC + LAG2))
-        def _():
-            b = c - LAG2
+        @pl.when((c >= LAG3) & (c < NC + LAG3))
+        def _():
+            b = c - LAG3
             wait_bytes(r2.at[b], s2_r.at[b])
             total = q2[b, second].astype(F32)
             for k in range(7):
@@ -251,15 +299,15 @@
                 device_id=dev3, device_id_type=MESH,
             ).start()
 
-        @pl.when(c >= LAG3)
-        def _():
-            b = c - LAG3
+        @pl.when(c >= LAG4)
+        def _():
+            b = c - LAG4
             wait_bytes(r3.at[b], s3_r.at[b])
             wg_ref[:, pl.ds(pl.multiple_of(b * DC, DC), DC)] = tot[b, zl] + r3[b]
 
         return 0
 
-    lax.fori_loop(0, NC + LAG3, step, 0)
+    lax.fori_loop(0, NC + LAG4, step, 0)
 
     wait_bytes(gate_in.at[pl.ds(0, NE - 1)], gr.at[0])
     wait_bytes(back_in.at[pl.ds(0, NE - 1)], ret_r.at[0])
@@ -275,7 +323,8 @@
 
     def settle(c, _):
         wait_bytes(send.at[c, pl.ds(0, NE - 1)], fwd_s.at[c])
-        wait_bytes(part.at[c, pl.ds(0, 7)], s1_s.at[c])
+        wait_bytes(part.at[c, pl.ds(0, 5)], leaf_s.at[c])
+        wait_bytes(mid.at[c], mid_s.at[c])
         wait_bytes(q2.at[c, pl.ds(0, 7)], s2_s.at[c])
         wait_bytes(tot.at[c, 0], s3_s.at[c])
         return 0
@@ -287,7 +336,7 @@
 
 def body(grad_out, expert_ids, gate_probs, hidden_saved, w_down):
     vmem = pl.BlockSpec(memory_space=pltpu.VMEM)
-    far = pl.BlockSpec(memory_space=pl.ANY)
+    far = pl.BlockSpec(memory_space=pltpu.HBM)
     dma = pltpu.SemaphoreType.DMA
     gh, gg, wg = pl.pallas_call(
         kernel,
@@ -296,9 +345,12 @@
             jax.ShapeDtypeStruct((2, TOK), F32),
             jax.ShapeDtypeStruct((8, D), F32),
         ),
-        in_specs=[vmem, vmem, vmem, far, far],
+        in_specs=[far] * 5,
         out_specs=(vmem, vmem, vmem),
         scratch_shapes=[
+            pltpu.VMEM((2, TOK), jnp.int32),
+            pltpu.VMEM((2, TOK), BF16),
+            pltpu.VMEM((TOK, D), BF16),
             pltpu.VMEM((ROWS, FF), BF16),
             pltpu.VMEM((FF, D), BF16),
             pltpu.VMEM((ROWS, TOK), BF16),
@@ -308,7 +360,9 @@
             pltpu.VMEM((NC, NE, 2 * CAP, H), BF16),
             pltpu.VMEM((ROWS, FF), F32),
             pltpu.VMEM((NC, 8, 96, DC), BF16),
-            pltpu.VMEM((NC, 7, 96, DC), BF16),
+            pltpu.VMEM((NC, 3, 96, DC), BF16),
+            pltpu.VMEM((NC, 2, 96, DC), BF16),
+            pltpu.VMEM((NC, 4, 96, DC), BF16),
             pltpu.VMEM((NC, 8, 16, DC), BF16),
             pltpu.VMEM((NC, 7, 16, DC), BF16),
             pltpu.VMEM((NC, 2, 8, DC), F32),
@@ -317,13 +371,12 @@
             pltpu.VMEM((NE, 2 * CAP, FH), BF16),
             pltpu.VMEM((NE, 8, 128), F32),
             pltpu.VMEM((NE, 8, 128), F32),
-            dma((2,)),
-            dma((NC,)), dma((NC,)), dma((NC,)), dma((NC,)),
-            dma((NC,)), dma((NC,)), dma((NC,)), dma((NC,)),
+            dma((5,)),
+            *[dma((NC,))] * 10,
             dma((1,)), dma((1,)), dma((1,)), dma((1,)),
         ],
         compiler_params=pltpu.CompilerParams(
-            collective_id=0, has_side_effects=True, vmem_limit_bytes=48 * 2**20
+            collective_id=0, has_side_effects=True, vmem_limit_bytes=533 * 2**20 // 10
         ),
         name="routed_backward",
     )(

time: 91.2 us -> 82.7 us (0.907)
  the two profiles are of different devices: /device:TPU:16 before, /device:TPU:2 now
where the time goes in v2:
time: 82.7 us; the launch traced here: 82.5 us
  Pallas kernels  78.2 us (95%)
  local copies, waits for them, and re-layouts  3.15 us (4%)
    pallas_call x1, Pallas kernels, body(): pl.pallas_call(kernel, out_shape=(jax.ShapeDtypeStruct((2, TOK, FF), BF16...  78.2 us
    unnamed x6, local copies, waits for them, and re-layouts  3.15 us

profile of v2, /device:TPU:2, one launch (start us, length us, event | category | flops | bytes accessed | tf_op | source)
XLA Modules:
  0.0 82.5 jit_solution(6964528378377130574)
XLA Ops:
  0.6 0.0 copy-start
  0.6 0.7 copy-done
  1.3 0.0 copy-start.1
  1.3 0.7 copy-done.1
  2.0 78.2 %routed_backward.1 = (bf16[2,128,768]{2,1,0:T(8,128)(2,1)S(1)}, f32[2,128]{1,0:T(2,128)S(1)}, f32[8,2048]{1,0:T(8,128)S(1)}) custom-call(s32[2,128]{1,0:T(2,128)S(1)} %bitcast.10, bf16[2,128]{1,0:T(2,128)(2,1)S(1)} %bitcast.11, bf16[128,2048]{1,0:T(8,128)(2,1)} %go_hbm.1, bf16[320,768]{1,0:T(8,128)(2,1)} %bitcast.13, bf16[768,2048]{1,0:T(8,128)(2,1)} %bitcast.12), custom_call_target="tpu_custom_call" | custom-call | tf_op jit(solution)/shard_map/routed_backward/pallas_call | solution.py:341
  80.2 1.2 %copy.8 = bf16[128,2,768]{2,1,0:T(2,128)(2,1)} copy(bf16[128,2,768]{2,0,1:T(8,128)(2,1)S(1)} %bitcast.9) | data formatting | bytes 786432
  81.3 0.5 convert_bitcast_fusion
  81.8 0.7 copy.9
  (1 shorter events, 0.0 us)
Async XLA Ops:
  0.6 0.7 copy-start
  1.3 0.7 copy-start.1

commit v3 on v2

--- a/solution.py
+++ b/solution.py
@@ -15,7 +15,7 @@
 DC = D // NC
 H = DC // 2
 FH = FF // 2
-NEAR, FAR = 2, 3
+NEAR, FAR = 2, 2
 LAG1, LAG2, LAG3, LAG4 = 1, 3, 5, 8
 F32, BF16 = jnp.float32, jnp.bfloat16
 NT = (((1,), (1,)), ((), ()))
@@ -143,9 +143,7 @@
     def prepare(c, _):
         dispatch(c)
 
-        @pl.when(c < FAR)
-        def _():
-            forward(c, (2,))
+        forward(c, (2,))
 
         @pl.when(c < NEAR)
         def _():
@@ -153,16 +151,7 @@
 
         return 0
 
-    lax.fori_loop(1, NC, prepare, 0)
-
-    eye = (
-        lax.broadcasted_iota(jnp.int32, (TOK, TOK), 0) == lax.broadcasted_iota(jnp.int32, (TOK, TOK), 1)
-    )
-    eye = jnp.where(eye, 1.0, 0.0).astype(BF16)
-    for k in range(2):
-        picked[k] = lax.dot_general(
-            eye, spots[k].astype(BF16), NT, preferred_element_type=F32
-        ).astype(BF16)
+    lax.fori_loop(1, FAR, prepare, 0)
 
     j = lax.broadcasted_iota(jnp.int32, (FF, 1), 0)
     major = (j * 683) >> 16
@@ -185,6 +174,10 @@
     def step(c, _):
         @pl.when(c < NC)
         def _():
+            @pl.when(c + FAR < NC)
+            def _():
+                dispatch(c + FAR)
+
             wait_bytes(recv.at[c, pl.ds(0, NE - 1)], fwd_r.at[c])
 
             @pl.when(c + FAR < NC)
@@ -304,6 +297,18 @@
             b = c - LAG4
             wait_bytes(r3.at[b], s3_r.at[b])
             wg_ref[:, pl.ds(pl.multiple_of(b * DC, DC), DC)] = tot[b, zl] + r3[b]
+
+        @pl.when(c == 2)
+        def _():
+            eye = (
+                lax.broadcasted_iota(jnp.int32, (TOK, TOK), 0)
+                == lax.broadcasted_iota(jnp.int32, (TOK, TOK), 1)
+            )
+            eye = jnp.where(eye, 1.0, 0.0).astype(BF16)
+            for k in range(2):
+                picked[k] = lax.dot_general(
+                    eye, spots[k].astype(BF16), NT, preferred_element_type=F32
+                ).astype(BF16)
 
         return 0
 

time: 82.7 us -> 81.1 us (0.981)
  the two profiles are of different devices: /device:TPU:2 before, /device:TPU:4 now
where the time goes in v3:
time: 81.1 us; the launch traced here: 80.9 us
  Pallas kernels  76.6 us (94%)
  local copies, waits for them, and re-layouts  3.15 us (4%)
    pallas_call x1, Pallas kernels, body(): pl.pallas_call(kernel, out_shape=(jax.ShapeDtypeStruct((2, TOK, FF), BF16...  76.6 us
    unnamed x6, local copies, waits for them, and re-layouts  3.15 us

profile of v3, /device:TPU:4, one launch (start us, length us, event | category | flops | bytes accessed | tf_op | source)
XLA Modules:
  0.0 80.9 jit_solution(8071435135975491367)
XLA Ops:
  0.6 0.0 copy-start
  0.6 0.7 copy-done
  1.3 0.0 copy-start.1
  1.3 0.7 copy-done.1
  2.0 76.6 %routed_backward.1 = (bf16[2,128,768]{2,1,0:T(8,128)(2,1)S(1)}, f32[2,128]{1,0:T(2,128)S(1)}, f32[8,2048]{1,0:T(8,128)S(1)}) custom-call(s32[2,128]{1,0:T(2,128)S(1)} %bitcast.10, bf16[2,128]{1,0:T(2,128)(2,1)S(1)} %bitcast.11, bf16[128,2048]{1,0:T(8,128)(2,1)} %go_hbm.1, bf16[320,768]{1,0:T(8,128)(2,1)} %bitcast.13, bf16[768,2048]{1,0:T(8,128)(2,1)} %bitcast.12), custom_call_target="tpu_custom_call" | custom-call | tf_op jit(solution)/shard_map/routed_backward/pallas_call | solution.py:346
  78.6 1.2 %copy.8 = bf16[128,2,768]{2,1,0:T(2,128)(2,1)} copy(bf16[128,2,768]{2,0,1:T(8,128)(2,1)S(1)} %bitcast.9) | data formatting | bytes 786432
  79.7 0.5 convert_bitcast_fusion
  80.2 0.7 copy.9
  (1 shorter events, 0.0 us)
Async XLA Ops:
  0.6 0.7 copy-start
  1.3 0.7 copy-start.1
